TPU v7x, 32 devices: a whole 2x2x4 slice. The times are simulated.
32 devices in a mesh: band: 4 (over y, x), lon: 8 (over z, core).
Axes of the slice: x: 2, y: 2, z: 4, core: 2. Of those that a mesh axis runs over, the one named last changes fastest.
Arguments:
- members: bfloat16 [1536, 48, 256], P(('band', 'lon')), may hold values from -6 to 6
- obs_perts: bfloat16 [1536, 32, 256], P(('band', 'lon')), may hold values from -6 to 6
- innovations: bfloat16 [1536, 32], P(('band', 'lon')), may hold values from -12 to 12
- lists: int32 [256, 64], P(('band', 'lon')), may hold values from 0 to 1535, as said below
- placement: int32 [1536], replicated, may hold values from 0 to 1535, as said below
- obs_taper: float32 [256, 64, 32], P(('band', 'lon')), may hold values from 0.01 to 0.2
- state_taper: float32 [256, 64], P(('band', 'lon')), may hold values from 0.2 to 1
Outputs:
- analysis: bfloat16 [1536, 48, 256], P(('band', 'lon'))
Inputs may be any that keep to these rules, and one draw needn't show every extreme that they name: `lists`: number the groups of 8 consecutive regions like the devices (band index times the lon count plus lon index) and call row // 48 a row's device. A group's entries name only blocks on the devices at band offset -1, 0 or 1 and lon offset -1, 0 or 1 (lon taken cyclically) from the group's own; from each such device that exists they name exactly 16 distinct blocks; every region names all 16 blocks of its own device; the 64 entries of one region are distinct. `placement`: A permutation of the block ids.
All inputs are finite; a program needn't handle non-finite values. Where the computation divides by a largest or mean magnitude, that divisor is 1e-20 or more.
Results may differ from a plain program's by a relative error of at most 0.0055.
Values may be sent and summed in bfloat16 or wider, within the bound.
A program may use at most 128 MiB of HBM per device.

v0:
```python
import jax
import jax.numpy as jnp
from jax import lax
from jax.sharding import PartitionSpec as P

NS_ITERS = 5
CAP = 16


def from_behind(block, axis, distance):
    devices = range(lax.axis_size(axis))
    route = [(i - distance, i) for i in devices if i - distance in devices]
    return lax.ppermute(block, axis, route)


def shifted(block, axis, distance):
    devices = range(lax.axis_size(axis))
    route = [((i - distance) % len(devices), i) for i in devices]
    return lax.ppermute(block, axis, route)


def inverse_root(matrix, identity):
    current = matrix
    estimate = identity
    for iteration in range(NS_ITERS):
        factor = 1.5 * identity - 0.5 * jnp.dot(estimate, current, precision=lax.Precision.HIGHEST)
        current = jnp.dot(current, factor, precision=lax.Precision.HIGHEST)
        estimate = jnp.dot(factor, estimate, precision=lax.Precision.HIGHEST)
    return estimate


def region_mix(obs_float, innov_float, slot_weights, ensemble):
    identity = jnp.eye(ensemble, dtype=jnp.float32)
    gram_matrix = jnp.einsum(
        "jpk,jpl->kl",
        obs_float * slot_weights[:, :, None],
        obs_float,
        precision=lax.Precision.HIGHEST,
    )
    projection = jnp.einsum(
        "jp,jpk->k", slot_weights * innov_float, obs_float, precision=lax.Precision.HIGHEST
    )
    system = (ensemble - 1.0) * identity + gram_matrix
    scale_top = jnp.max(jnp.sum(jnp.abs(system), axis=1))
    inverse_sqrt = inverse_root(system / scale_top, identity) / jnp.sqrt(scale_top)
    halfway = jnp.dot(inverse_sqrt, projection, precision=lax.Precision.HIGHEST)
    mean_weights = jnp.dot(inverse_sqrt, halfway, precision=lax.Precision.HIGHEST)
    mixing = jnp.sqrt(ensemble - 1.0) * inverse_sqrt - identity + mean_weights[:, None]
    return mixing.astype(jnp.bfloat16)


def spread(layered, mover, direction, axis_pos):
    portions = []
    for ordinal in range(3):
        offset = direction * (ordinal - 1)
        if axis_pos == 0:
            portion = layered[ordinal]
        else:
            portion = layered[:, ordinal]
        portions.append(portion if offset == 0 else mover(portion, offset))
    return jnp.stack(portions, axis=axis_pos)


def route(layered, band_mover, lon_mover, direction):
    return spread(spread(layered, band_mover, direction, 0), lon_mover, direction, 1)


def asking_band(portion, offset):
    return from_behind(portion, "band", offset)


def asking_lon(portion, offset):
    return shifted(portion, "lon", offset)


def fetching_band(portion, offset):
    return from_behind(portion, "band", offset)


def fetching_lon(portion, offset):
    return shifted(portion, "lon", offset)


def returning_band(portion, offset):
    return from_behind(portion, "band", offset)


def returning_lon(portion, offset):
    return shifted(portion, "lon", offset)


def pick_rows(selector, source):
    flat = source.reshape(source.shape[0], -1)
    picked = jnp.dot(selector, flat, preferred_element_type=jnp.float32)
    return picked.astype(jnp.bfloat16).reshape((selector.shape[0],) + source.shape[1:])


def local(members, obs_perts, innovations, lists, placement, obs_taper, state_taper):
    lon_count = lax.axis_size("lon")
    band_here = lax.axis_index("band")
    lon_here = lax.axis_index("lon")
    block_count, state_rows, ensemble = members.shape
    obs_rows = obs_perts.shape[1]
    region_count, list_len = lists.shape
    entries = region_count * list_len
    pool_size = 9 * CAP
    row_ids = jnp.take(placement, lists.reshape(-1), axis=0)
    holder = row_ids // block_count
    band_step = holder // lon_count - band_here
    lon_step = (holder % lon_count - lon_here + 1) % lon_count - 1
    neighbour = (band_step + 1) * 3 + lon_step + 1
    inside_row = row_ids % block_count
    positions = jnp.arange(entries, dtype=jnp.int32)
    matching = row_ids[:, None] == row_ids[None, :]
    leading = jnp.logical_not(jnp.any(matching & (positions[None, :] < positions[:, None]), axis=1))
    class_hot = (
        (neighbour[:, None] == jnp.arange(9, dtype=jnp.int32)[None, :]) & leading[:, None]
    ).astype(jnp.int32)
    ordinal_in = jnp.sum((jnp.cumsum(class_hot, axis=0) - class_hot) * class_hot, axis=1)
    lead_slot = neighbour * CAP + ordinal_in
    slot_of = jnp.max(jnp.where(matching & leading[None, :], lead_slot[None, :], 0), axis=1)
    pool_ids = jnp.arange(pool_size, dtype=jnp.int32)
    entry_hot = slot_of[:, None] == pool_ids[None, :]
    wanted = jnp.sum(jnp.where(entry_hot, (inside_row + 1)[:, None], 0), axis=0)
    requested = jnp.max(
        jnp.where(entry_hot & leading[:, None], (inside_row + 1)[:, None], 0), axis=0
    )
    requested = jnp.minimum(requested, wanted)
    received = route(requested.reshape(3, 3, CAP), asking_band, asking_lon, 1)
    received_flat = received.reshape(-1)
    chosen = jnp.maximum(received_flat - 1, 0)
    block_ids = jnp.arange(block_count, dtype=jnp.int32)
    selector = (chosen[:, None] == block_ids[None, :]).astype(jnp.bfloat16)
    padded_innov = jnp.pad(innovations[:, None, :], ((0, 0), (0, 0), (0, ensemble - obs_rows)))
    payload = jnp.concatenate([members, obs_perts, padded_innov], axis=1)
    carried = state_rows + obs_rows + 1
    outgoing = pick_rows(selector, payload).reshape(3, 3, CAP, carried, ensemble)
    arrived = route(outgoing, fetching_band, fetching_lon, -1).reshape(pool_size, carried, ensemble)
    state_pool = arrived[:, :state_rows]
    obs_pool = arrived[:, state_rows : state_rows + obs_rows]
    innov_pool = arrived[:, state_rows + obs_rows, :obs_rows]
    obs_float = obs_pool.astype(jnp.float32)
    innov_float = innov_pool.astype(jnp.float32)
    slot_hot = entry_hot.astype(jnp.float32).reshape(region_count, list_len, pool_size)

    def one_region(region, increment):
        region_hot = lax.dynamic_index_in_dim(slot_hot, region, 0, keepdims=False)
        weights = lax.dynamic_index_in_dim(obs_taper, region, 0, keepdims=False)
        tapers = lax.dynamic_index_in_dim(state_taper, region, 0, keepdims=False)
        slot_weights = jnp.dot(region_hot.T, weights, precision=lax.Precision.HIGHEST)
        slot_tapers = jnp.dot(tapers, region_hot, precision=lax.Precision.HIGHEST)
        mixing = region_mix(obs_float, innov_float, slot_weights, ensemble)
        portion = jnp.einsum("qsk,kl->qsl", state_pool, mixing, preferred_element_type=jnp.float32)
        portion = lax.optimization_barrier(
            (portion * slot_tapers[:, None, None]).astype(jnp.bfloat16)
        )
        return increment + portion.astype(jnp.float32)

    increment = lax.fori_loop(
        0, region_count, one_region, jnp.zeros((pool_size, state_rows, ensemble), jnp.float32)
    )
    outgoing_sum = increment.astype(jnp.bfloat16).reshape(3, 3, CAP, state_rows, ensemble)
    returned = route(outgoing_sum, returning_band, returning_lon, 1).reshape(
        pool_size, state_rows * ensemble
    )
    target_hot = (
        jnp.arange(1, block_count + 1, dtype=jnp.int32)[:, None] == received_flat[None, :]
    ).astype(jnp.bfloat16)
    summed = jnp.dot(target_hot, returned, preferred_element_type=jnp.float32)
    summed = summed.reshape(block_count, state_rows, ensemble)
    return (members.astype(jnp.float32) + summed).astype(jnp.bfloat16)


def solution(mesh):
    in_specs = (
        P(("band", "lon"), None, None),
        P(("band", "lon"), None, None),
        P(("band", "lon"), None),
        P(("band", "lon"), None),
        P(),
        P(("band", "lon"), None, None),
        P(("band", "lon"), None),
    )
    out_specs = P(("band", "lon"), None, None)
    return jax.shard_map(local, mesh=mesh, in_specs=in_specs, out_specs=out_specs, check_vma=False)
```

profile of v0, /device:TPU:6, one launch (start us, length us, event | category | flops | bytes accessed | tf_op | source)
XLA Modules:
  0.0 577.0 jit_solution(735761596687838438)
XLA Ops:
  33.5 5.6 collective-permute-start.5
  47.7 29.5 %collective-permute-done.5 = bf16[3,16,81,256]{3,1,2,0:T(8,128)(2,1)} collective-permute-done((bf16[3,16,81,256]{3,1,2,0:T(8,128)(2,1)}, bf16[3,16,81,256]{3,1,2,0:T(8,128)(2,1)}, u32[]{:S(2)}, u32[]{:S(2)}) %collective-permute-start.5) | collective-permute-done | bytes 1990688 | tf_op jit(solution)/shard_map/ppermute | solution.py:13
  79.5 43.1 %collective-permute-done.4 = bf16[3,16,81,256]{3,1,2,0:T(8,128)(2,1)} collective-permute-done((bf16[3,16,81,256]{3,1,2,0:T(8,128)(2,1)}, bf16[3,16,81,256]{3,1,2,0:T(8,128)(2,1)}, u32[]{:S(2)}, u32[]{:S(2)}) %collective-permute-start.4) | collective-permute-done | bytes 1990688 | tf_op jit(solution)/shard_map/ppermute | solution.py:13
  134.7 40.0 %collective-permute-done.7 = bf16[3,16,81,256]{3,1,2,0:T(8,128)(2,1)} collective-permute-done((bf16[3,16,81,256]{3,1,2,0:T(8,128)(2,1)}, bf16[3,16,81,256]{3,1,2,0:T(8,128)(2,1)}, u32[]{:S(2)}, u32[]{:S(2)}) %collective-permute-start.7) | collective-permute-done | bytes 1990688 | tf_op jit(solution)/shard_map/ppermute | solution.py:19
  186.9 298.3 %while.14 = (s32[]{:T(128)}, f32[144,48,256]{2,0,1:T(8,128)}, f32[8,64,144]{2,1,0:T(8,128)}, f32[8,64,32]{1,2,0:T(8,128)}, f32[144,32,256]{2,0,1:T(8,128)}, /*in...) while((s32[]{:T(128)}, f32[144,48,256]{2,0,1:T(8,128)}, ...), condition=%wide.region_10.11_spmd.clone, body=%wide.region_7.10_spmd.clone.sunk | while | flops 7380189696 | bytes 60170028 | solution.py:159
  187.9 12.0 %abs_reduce_fusion.2 = (f32[256]{0:T(256)S(1)}, f32[256,256]{0,1:T(8,128)S(1)}) fusion(f32[144,32,256]{2,0,1:T(8,128)} %get-tuple-element.301, f32[144,32]{0,1:T(8,128)S(1)} %fusion.215), kind=kOutput, calls=%fused_computation.23.clone.1 | convolution fusion | flops 3625385728 | bytes 5000192 | tf_op jit(solution)/shard_map/while/body/eval_jaxpr/jpk,jpl->kl/dot_general | solution.py:34
  210.9 4.1 convolution_bitcast_fusion.4
  222.6 12.0 %abs_reduce_fusion.2 = (f32[256]{0:T(256)S(1)}, f32[256,256]{0,1:T(8,128)S(1)}) fusion(f32[144,32,256]{2,0,1:T(8,128)} %get-tuple-element.301, f32[144,32]{0,1:T(8,128)S(1)} %fusion.215), kind=kOutput, calls=%fused_computation.23.clone.1 | convolution fusion | flops 3625385728 | bytes 5000192 | tf_op jit(solution)/shard_map/while/body/eval_jaxpr/jpk,jpl->kl/dot_general | solution.py:34
  252.2 6.9 %select_add_fusion.2 = f32[144,48,256]{2,0,1:T(8,128)} fusion(f32[144,48,256]{2,0,1:T(8,128)} %get-tuple-element.287, bf16[144,48,256]{2,0,1:T(8,128)(2,1)S(1)} %fusion.230, pred[]{:T(512)S(6)} %compare.41), kind=kLoop, calls=%fused_computation.1.clone.1 | loop fusion | flops 5308416 | bytes 17694720 | tf_op jit(solution)/shard_map/while/body/eval_jaxpr/add | solution.py:157
  260.2 12.0 %abs_reduce_fusion.2 = (f32[256]{0:T(256)S(1)}, f32[256,256]{0,1:T(8,128)S(1)}) fusion(f32[144,32,256]{2,0,1:T(8,128)} %get-tuple-element.301, f32[144,32]{0,1:T(8,128)S(1)} %fusion.215), kind=kOutput, calls=%fused_computation.23.clone.1 | convolution fusion | flops 3625385728 | bytes 5000192 | tf_op jit(solution)/shard_map/while/body/eval_jaxpr/jpk,jpl->kl/dot_general | solution.py:34
  283.1 4.1 convolution_bitcast_fusion.4
  289.9 6.9 %select_add_fusion.2 = f32[144,48,256]{2,0,1:T(8,128)} fusion(f32[144,48,256]{2,0,1:T(8,128)} %get-tuple-element.287, bf16[144,48,256]{2,0,1:T(8,128)(2,1)S(1)} %fusion.230, pred[]{:T(512)S(6)} %compare.41), kind=kLoop, calls=%fused_computation.1.clone.1 | loop fusion | flops 5308416 | bytes 17694720 | tf_op jit(solution)/shard_map/while/body/eval_jaxpr/add | solution.py:157
  297.8 12.0 %abs_reduce_fusion.2 = (f32[256]{0:T(256)S(1)}, f32[256,256]{0,1:T(8,128)S(1)}) fusion(f32[144,32,256]{2,0,1:T(8,128)} %get-tuple-element.301, f32[144,32]{0,1:T(8,128)S(1)} %fusion.215), kind=kOutput, calls=%fused_computation.23.clone.1 | convolution fusion | flops 3625385728 | bytes 5000192 | tf_op jit(solution)/shard_map/while/body/eval_jaxpr/jpk,jpl->kl/dot_general | solution.py:34
  320.8 4.1 convolution_bitcast_fusion.4
  327.5 6.9 %select_add_fusion.2 = f32[144,48,256]{2,0,1:T(8,128)} fusion(f32[144,48,256]{2,0,1:T(8,128)} %get-tuple-element.287, bf16[144,48,256]{2,0,1:T(8,128)(2,1)S(1)} %fusion.230, pred[]{:T(512)S(6)} %compare.41), kind=kLoop, calls=%fused_computation.1.clone.1 | loop fusion | flops 5308416 | bytes 17694720 | tf_op jit(solution)/shard_map/while/body/eval_jaxpr/add | solution.py:157
  335.5 12.0 %abs_reduce_fusion.2 = (f32[256]{0:T(256)S(1)}, f32[256,256]{0,1:T(8,128)S(1)}) fusion(f32[144,32,256]{2,0,1:T(8,128)} %get-tuple-element.301, f32[144,32]{0,1:T(8,128)S(1)} %fusion.215), kind=kOutput, calls=%fused_computation.23.clone.1 | convolution fusion | flops 3625385728 | bytes 5000192 | tf_op jit(solution)/shard_map/while/body/eval_jaxpr/jpk,jpl->kl/dot_general | solution.py:34
  358.4 4.1 convolution_bitcast_fusion.4
  365.2 6.9 %select_add_fusion.2 = f32[144,48,256]{2,0,1:T(8,128)} fusion(f32[144,48,256]{2,0,1:T(8,128)} %get-tuple-element.287, bf16[144,48,256]{2,0,1:T(8,128)(2,1)S(1)} %fusion.230, pred[]{:T(512)S(6)} %compare.41), kind=kLoop, calls=%fused_computation.1.clone.1 | loop fusion | flops 5308416 | bytes 17694720 | tf_op jit(solution)/shard_map/while/body/eval_jaxpr/add | solution.py:157
  373.1 12.0 %abs_reduce_fusion.2 = (f32[256]{0:T(256)S(1)}, f32[256,256]{0,1:T(8,128)S(1)}) fusion(f32[144,32,256]{2,0,1:T(8,128)} %get-tuple-element.301, f32[144,32]{0,1:T(8,128)S(1)} %fusion.215), kind=kOutput, calls=%fused_computation.23.clone.1 | convolution fusion | flops 3625385728 | bytes 5000192 | tf_op jit(solution)/shard_map/while/body/eval_jaxpr/jpk,jpl->kl/dot_general | solution.py:34
  396.1 4.1 convolution_bitcast_fusion.4
  402.8 6.9 %select_add_fusion.2 = f32[144,48,256]{2,0,1:T(8,128)} fusion(f32[144,48,256]{2,0,1:T(8,128)} %get-tuple-element.287, bf16[144,48,256]{2,0,1:T(8,128)(2,1)S(1)} %fusion.230, pred[]{:T(512)S(6)} %compare.41), kind=kLoop, calls=%fused_computation.1.clone.1 | loop fusion | flops 5308416 | bytes 17694720 | tf_op jit(solution)/shard_map/while/body/eval_jaxpr/add | solution.py:157
  410.8 12.0 %abs_reduce_fusion.2 = (f32[256]{0:T(256)S(1)}, f32[256,256]{0,1:T(8,128)S(1)}) fusion(f32[144,32,256]{2,0,1:T(8,128)} %get-tuple-element.301, f32[144,32]{0,1:T(8,128)S(1)} %fusion.215), kind=kOutput, calls=%fused_computation.23.clone.1 | convolution fusion | flops 3625385728 | bytes 5000192 | tf_op jit(solution)/shard_map/while/body/eval_jaxpr/jpk,jpl->kl/dot_general | solution.py:34
  433.7 4.1 convolution_bitcast_fusion.4
  440.5 6.9 %select_add_fusion.2 = f32[144,48,256]{2,0,1:T(8,128)} fusion(f32[144,48,256]{2,0,1:T(8,128)} %get-tuple-element.287, bf16[144,48,256]{2,0,1:T(8,128)(2,1)S(1)} %fusion.230, pred[]{:T(512)S(6)} %compare.41), kind=kLoop, calls=%fused_computation.1.clone.1 | loop fusion | flops 5308416 | bytes 17694720 | tf_op jit(solution)/shard_map/while/body/eval_jaxpr/add | solution.py:157
  448.4 12.0 %abs_reduce_fusion.2 = (f32[256]{0:T(256)S(1)}, f32[256,256]{0,1:T(8,128)S(1)}) fusion(f32[144,32,256]{2,0,1:T(8,128)} %get-tuple-element.301, f32[144,32]{0,1:T(8,128)S(1)} %fusion.215), kind=kOutput, calls=%fused_computation.23.clone.1 | convolution fusion | flops 3625385728 | bytes 5000192 | tf_op jit(solution)/shard_map/while/body/eval_jaxpr/jpk,jpl->kl/dot_general | solution.py:34
  471.4 4.1 convolution_bitcast_fusion.4
  478.1 6.9 %select_add_fusion.2 = f32[144,48,256]{2,0,1:T(8,128)} fusion(f32[144,48,256]{2,0,1:T(8,128)} %get-tuple-element.287, bf16[144,48,256]{2,0,1:T(8,128)(2,1)S(1)} %fusion.230, pred[]{:T(512)S(6)} %compare.41), kind=kLoop, calls=%fused_computation.1.clone.1 | loop fusion | flops 5308416 | bytes 17694720 | tf_op jit(solution)/shard_map/while/body/eval_jaxpr/add | solution.py:157
  493.6 20.5 %collective-permute-done.8 = bf16[3,16,48,256]{3,2,1,0:T(8,128)(2,1)S(1)} collective-permute-done((bf16[3,16,48,256]{3,2,1,0:T(8,128)(2,1)S(1)}, bf16[3,16,48,256]{3,2,1,0:T(8,128)(2,1)S(1)}, u32[]{:S(2)}, u32[]{:S(2)}) %collective-permute-start.8) | collective-permute-done | bytes 1179680 | tf_op jit(solution)/shard_map/ppermute | solution.py:13
  514.1 26.0 %collective-permute-done.9 = bf16[3,16,48,256]{3,2,1,0:T(8,128)(2,1)S(1)} collective-permute-done((bf16[3,16,48,256]{3,2,1,0:T(8,128)(2,1)S(1)}, bf16[3,16,48,256]{3,2,1,0:T(8,128)(2,1)S(1)}, u32[]{:S(2)}, u32[]{:S(2)}) %collective-permute-start.9) | collective-permute-done | bytes 1179680 | tf_op jit(solution)/shard_map/ppermute | solution.py:13
  540.8 5.3 collective-permute-start.10
  546.1 22.2 %collective-permute-done.10 = bf16[3,16,48,256]{3,2,1,0:T(8,128)(2,1)S(1)} collective-permute-done((bf16[3,16,48,256]{3,2,1,0:T(8,128)(2,1)S(1)}, bf16[3,16,48,256]{3,2,1,0:T(8,128)(2,1)S(1)}, u32[]{:S(2)}, u32[]{:S(2)}) %collective-permute-start.10) | collective-permute-done | bytes 1179680 | tf_op jit(solution)/shard_map/ppermute | solution.py:19
  568.3 4.2 collective-permute-done.11
  (287 shorter events, 199.5 us)
Async XLA Ops:
  0.0 2.4 copy-start
  0.0 12.1 %copy-start.5 = (bf16[48,32]{0,1:T(8,128)(2,1)S(1)}, bf16[48,32]{0,1:T(8,128)(2,1)}, u32[]{:S(2)}) copy-start(bf16[48,32]{0,1:T(8,128)(2,1)} %param.11) | copy-start | bytes 9220
  0.0 12.2 %copy-start.3 = (bf16[48,48,256]{2,1,0:T(8,128)(2,1)S(1)}, bf16[48,48,256]{2,1,0:T(8,128)(2,1)}, u32[]{:S(2)}) copy-start(bf16[48,48,256]{2,1,0:T(8,128)(2,1)} %param.9) | copy-start | bytes 3538948
  8.3 7.0 %collective-permute-start = (s32[3,16]{1,0:T(4,128)S(1)}, s32[3,16]{1,0:T(4,128)S(1)}, u32[]{:S(2)}, u32[]{:S(2)}) collective-permute-start(s32[3,16]{1,0:T(4,128)S(1)} %slice.97), channel_id=1, source_target_pairs={{8,0},{16,8},{24,16},{9,1},{17,9},{25,17},{10,2},{18,10},{26,18},{... | collective-permute-start | bytes 584 | tf_op jit(solution)/shard_map/ppermute | solution.py:13
  10.8 5.5 collective-permute-start.1
  16.3 3.1 collective-permute-start.2
  18.1 4.8 collective-permute-start.3
  33.5 43.7 %collective-permute-start.5 = (bf16[3,16,81,256]{3,1,2,0:T(8,128)(2,1)}, bf16[3,16,81,256]{3,1,2,0:T(8,128)(2,1)}, u32[]{:S(2)}, u32[]{:S(2)}) collective-permute-start(bf16[3,16,81,256]{3,1,2,0:T(8,128)(2,1)} %copy.141), channel_id=1, source_target_pairs={{8,0},{16,8},{24,16},{9,1},{17,9},{25,17},{10,2},{18,10},{26,18},{... | collective-permute-start | bytes 5971976 | tf_op jit(solution)/shard_map/ppermute | solution.py:13
  43.6 79.1 %collective-permute-start.4 = (bf16[3,16,81,256]{3,1,2,0:T(8,128)(2,1)}, bf16[3,16,81,256]{3,1,2,0:T(8,128)(2,1)}, u32[]{:S(2)}, u32[]{:S(2)}) collective-permute-start(bf16[3,16,81,256]{3,1,2,0:T(8,128)(2,1)} %copy.139), channel_id=1, source_target_pairs={{0,8},{8,16},{16,24},{1,9},{9,17},{17,25},{2,10},{10,18},{18,26},{... | collective-permute-start | bytes 5971976 | tf_op jit(solution)/shard_map/ppermute | solution.py:13
  128.0 46.7 %collective-permute-start.7 = (bf16[3,16,81,256]{3,1,2,0:T(8,128)(2,1)}, bf16[3,16,81,256]{3,1,2,0:T(8,128)(2,1)}, u32[]{:S(2)}, u32[]{:S(2)}) collective-permute-start(bf16[3,16,81,256]{3,1,2,0:T(8,128)(2,1)} %copy.145), channel_id=1, source_target_pairs={{1,0},{2,1},{3,2},{4,3},{5,4},{6,5},{7,6},{0,7},{9,8},{10,9},{11,1... | collective-permute-start | bytes 5971976 | tf_op jit(solution)/shard_map/ppermute | solution.py:19
  133.4 43.6 %collective-permute-start.6 = (bf16[3,16,81,256]{3,1,2,0:T(8,128)(2,1)}, bf16[3,16,81,256]{3,1,2,0:T(8,128)(2,1)}, u32[]{:S(2)}, u32[]{:S(2)}) collective-permute-start(bf16[3,16,81,256]{3,1,2,0:T(8,128)(2,1)} %copy.143), channel_id=1, source_target_pairs={{7,0},{0,1},{1,2},{2,3},{3,4},{4,5},{5,6},{6,7},{15,8},{8,9},{9,10... | collective-permute-start | bytes 5971976 | tf_op jit(solution)/shard_map/ppermute | solution.py:19
  210.9 5.6 copy-start.2
  245.5 5.6 copy-start.2
  283.1 5.6 copy-start.2
  320.8 5.6 copy-start.2
  358.4 5.6 copy-start.2
  396.1 5.6 copy-start.2
  433.7 5.6 copy-start.2
  471.4 5.6 copy-start.2
  489.3 24.8 %collective-permute-start.8 = (bf16[3,16,48,256]{3,2,1,0:T(8,128)(2,1)S(1)}, bf16[3,16,48,256]{3,2,1,0:T(8,128)(2,1)S(1)}, u32[]{:S(2)}, u32[]{:S(2)}) collective-permute-start(bf16[3,16,48,256]{3,2,1,0:T(8,128)(2,1)S(1)} %copy.149), channel_id=1, source_target_pairs={{8,0},{16,8},{24,16},{9,1},{17,9},{25,17},{10,2},{18,10},{26,18},{... | collective-permute-start | bytes 3538952 | tf_op jit(solution)/shard_map/ppermute | solution.py:13
  491.9 48.2 %collective-permute-start.9 = (bf16[3,16,48,256]{3,2,1,0:T(8,128)(2,1)S(1)}, bf16[3,16,48,256]{3,2,1,0:T(8,128)(2,1)S(1)}, u32[]{:S(2)}, u32[]{:S(2)}) collective-permute-start(bf16[3,16,48,256]{3,2,1,0:T(8,128)(2,1)S(1)} %copy.150), channel_id=1, source_target_pairs={{0,8},{8,16},{16,24},{1,9},{9,17},{17,25},{2,10},{10,18},{18,26},{... | collective-permute-start | bytes 3538952 | tf_op jit(solution)/shard_map/ppermute | solution.py:13
  540.8 27.5 %collective-permute-start.10 = (bf16[3,16,48,256]{3,2,1,0:T(8,128)(2,1)S(1)}, bf16[3,16,48,256]{3,2,1,0:T(8,128)(2,1)S(1)}, u32[]{:S(2)}, u32[]{:S(2)}) collective-permute-start(bf16[3,16,48,256]{3,2,1,0:T(8,128)(2,1)S(1)} %get-tuple-element.208), channel_id=1, source_target_pairs={{1,0},{2,1},{3,2},{4,3},{5,4},{6,5},{7,6},{0,7},{9,8},{10,9},{11,1... | collective-permute-start | bytes 3538952 | tf_op jit(solution)/shard_map/ppermute | solution.py:19
  546.1 26.4 %collective-permute-start.11 = (bf16[3,16,48,256]{3,2,1,0:T(8,128)(2,1)S(1)}, bf16[3,16,48,256]{3,2,1,0:T(8,128)(2,1)S(1)}, u32[]{:S(2)}, u32[]{:S(2)}) collective-permute-start(bf16[3,16,48,256]{3,2,1,0:T(8,128)(2,1)S(1)} %get-tuple-element.209), channel_id=1, source_target_pairs={{7,0},{0,1},{1,2},{2,3},{3,4},{4,5},{5,6},{6,7},{15,8},{8,9},{9,10... | collective-permute-start | bytes 3538952 | tf_op jit(solution)/shard_map/ppermute | solution.py:19
  572.5 1.3 copy-start.4
  573.8 3.0 copy-start.1
where the time goes:
time: 586 us; the launch traced here: 577 us
  matrix products  232 us (40%)
  waiting for transfers between devices  191 us (33%)
  other arithmetic  77.9 us (13%)
  local copies, waits for them, and re-layouts  43 us (7%)
  starting transfers between devices  25.2 us (4%)
  loops' own time  7.13 us (1%)
    ppermute x6, waiting for transfers between devices, from_behind(): return lax.ppermute(block, axis, route)  120 us
    dot_general x8, matrix products, region_mix(): jnp.einsum('jpk,jpl->kl', obs_float * slot_weights[:, :, None], obs_float...  96 us
    ppermute x6, waiting for transfers between devices, shifted(): return lax.ppermute(block, axis, route)  71.1 us
    add x8, other arithmetic, one_region(): return increment + portion.astype(jnp.float32)  52.6 us
    dot_general x8, matrix products, region_mix(): jnp.einsum('jp,jpk->k', slot_weights * innov_float, obs_float, precision=...  32.8 us
    dot_general x40, matrix products, inverse_root(): jnp.dot(estimate, current, precision=lax.Precision.HIGHEST)  26.9 us
    dot_general x40, matrix products, inverse_root(): estimate = jnp.dot(factor, estimate, precision=lax.Precision.HIGHEST)  22.2 us
    dot_general x32, matrix products, inverse_root(): current = jnp.dot(current, factor, precision=lax.Precision.HIGHEST)  20.1 us
  transfers between devices with their start and end apart: 12, of which 10 were waited for; matrix products, arithmetic and copies ran while one was open for 3% of the time, Pallas kernels for 0%

commit v1 on v0

v1 whole, which is shorter than its diff:
```python
import functools

import jax
import jax.numpy as jnp
from jax import lax
from jax.experimental import pallas as pl
from jax.experimental.pallas import tpu as pltpu
from jax.sharding import PartitionSpec as P

NS_ITERS = 5
CAP = 16
NEAR = 9
OWN = 4
MESH = pl.DeviceIdType.MESH
NT = (((1,), (1,)), ((), ()))


def peer_of(direction, band_count, lon_count):
    band = lax.axis_index("band") + direction // 3 - 1
    lon = lax.rem(lax.axis_index("lon") + lax.rem(direction, 3) - 1 + lon_count, lon_count)
    exists = (band >= 0) & (band < band_count)
    return exists, (band, lon)


def greet(band_count, lon_count):
    barrier = pltpu.get_barrier_semaphore()
    for direction in range(NEAR):
        if direction != OWN:
            exists, device = peer_of(direction, band_count, lon_count)

            @pl.when(exists)
            def _():
                pl.semaphore_signal(barrier, inc=1, device_id=device, device_id_type=MESH)

    band = lax.axis_index("band")
    beside = (band > 0).astype(jnp.int32) + (band < band_count - 1).astype(jnp.int32)
    pl.semaphore_wait(barrier, 2 + 3 * beside)


def copy_to(direction, source, landing, send_sem, recv_sem, device):
    return pltpu.make_async_remote_copy(
        src_ref=source.at[direction],
        dst_ref=landing.at[8 - direction],
        send_sem=send_sem.at[direction],
        recv_sem=recv_sem.at[8 - direction],
        device_id=device,
        device_id_type=MESH,
    )


def copy_from(direction, source, landing, send_sem, recv_sem, device):
    return pltpu.make_async_remote_copy(
        src_ref=source.at[direction],
        dst_ref=landing.at[direction],
        send_sem=send_sem.at[direction],
        recv_sem=recv_sem.at[direction],
        device_id=device,
        device_id_type=MESH,
    )


def ask_kernel(band_count, lon_count, ask_ref, got_ref, send_sem, recv_sem):
    peer = functools.partial(peer_of, band_count=band_count, lon_count=lon_count)
    greet(band_count, lon_count)
    for direction in range(NEAR):
        if direction == OWN:
            continue
        exists, device = peer(direction)

        @pl.when(exists)
        def _():
            copy_to(direction, ask_ref, got_ref, send_sem, recv_sem, device).start()

        @pl.when(jnp.logical_not(exists))
        def _():
            got_ref[direction] = jnp.full(got_ref.shape[1:], -1.0, jnp.float32)

    got_ref[OWN] = ask_ref[OWN]
    for direction in range(NEAR):
        if direction == OWN:
            continue
        exists, device = peer(direction)

        @pl.when(exists)
        def _():
            copy_from(direction, ask_ref, got_ref, send_sem, recv_sem, device).wait()


def analysis_kernel(
    band_count,
    lon_count,
    ids_ref,
    back_ref,
    hit_ref,
    taper_ref,
    members_ref,
    obs_ref,
    weight_ref,
    push_ref,
    out_ref,
    obs_out,
    obs_in,
    state_out,
    state_in,
    share_out,
    share_in,
    gram,
    turned,
    proj,
    mix,
    scaled,
    obs_send,
    obs_recv,
    state_send,
    state_recv,
    share_send,
    share_recv,
):
    peer = functools.partial(peer_of, band_count=band_count, lon_count=lon_count)
    blocks, state_rows, ensemble = members_ref.shape
    obs_rows = obs_ref.shape[1]
    regions = weight_ref.shape[1]

    def edge(i):
        return lax.rem(2 * i + 3, 8)

    def corner(i):
        return 2 * i + 2 * (i // 2)

    def each(order, body):
        def step(i, carry):
            direction = order(i)
            exists, device = peer(direction)

            @pl.when(exists)
            def _():
                body(direction, device)

            return carry

        lax.fori_loop(0, 4, step, 0)

    def pack_obs(direction, target):
        def one(i, carry):
            at = pl.multiple_of(i * obs_rows, obs_rows)
            target[direction, pl.ds(at, obs_rows), :] = obs_ref[ids_ref[direction, i]]
            return carry

        lax.fori_loop(0, CAP, one, 0)

    def pack_state(direction, target):
        def one(i, carry):
            target[direction, i] = members_ref[ids_ref[direction, i]]
            return carry

        lax.fori_loop(0, CAP, one, 0)

    greet(band_count, lon_count)

    def send_obs(direction, device):
        pack_obs(direction, obs_out)
        copy_to(direction, obs_out, obs_in, obs_send, obs_recv, device).start()

    each(corner, send_obs)
    each(edge, send_obs)
    pack_obs(OWN, obs_in)

    def clear(r, carry):
        gram[r] = jnp.zeros((ensemble, ensemble), jnp.float32)
        return carry

    lax.fori_loop(0, regions, clear, 0)
    proj[...] = jnp.zeros_like(proj)

    def add_gram(direction):
        turned[...] = obs_in[direction].astype(jnp.float32).T
        proj[...] += jnp.dot(
            push_ref[direction], obs_in[direction], preferred_element_type=jnp.float32
        )

        def one(r, carry):
            left = (turned[...] * weight_ref[direction, pl.ds(r, 1), :]).astype(jnp.bfloat16)
            gram[r] += jnp.dot(left, obs_in[direction], preferred_element_type=jnp.float32)
            return carry

        lax.fori_loop(0, regions, one, 0)

    def take_obs(direction, device):
        copy_from(direction, obs_out, obs_in, obs_send, obs_recv, device).wait()
        add_gram(direction)

    def fill_state(direction, device):
        pack_state(direction, state_out)

    def send_state(direction, device):
        copy_to(direction, state_out, state_in, state_send, state_recv, device).start()

    add_gram(OWN)
    each(corner, fill_state)
    each(edge, fill_state)
    pack_state(OWN, state_in)
    each(edge, take_obs)
    each(corner, send_state)
    each(edge, send_state)
    each(corner, take_obs)

    rows = lax.broadcasted_iota(jnp.int32, (ensemble, ensemble), 0)
    columns = lax.broadcasted_iota(jnp.int32, (ensemble, ensemble), 1)
    identity = (rows == columns).astype(jnp.float32)

    def dot(a, b):
        return jnp.dot(
            a.astype(jnp.bfloat16), b.astype(jnp.bfloat16), preferred_element_type=jnp.float32
        )

    def total(a):
        return jnp.sum(jnp.sum(a, axis=1, keepdims=True), axis=0, keepdims=True)

    def transform(r0, width):
        span = range(width)
        scale, lead, rest, gain, part = [], [], [], [], []
        for k in span:
            system = (ensemble - 1.0) * identity + gram[r0 + k]
            sums = jnp.sum(jnp.abs(system), axis=1, keepdims=True)
            top = jnp.max(sums, axis=0, keepdims=True)
            inside = identity - system / top
            middle = total(inside * identity) * (1.0 / ensemble)
            scale.append(top)
            lead.append(middle)
            rest.append(inside - middle * identity)
            gain.append(1.0 + 0.5 * middle)
            part.append(0.5 * rest[k])
        for _ in range(NS_ITERS - 1):
            square = [dot(rest[k], rest[k]) for k in span]
            square = [2.0 * lead[k] * rest[k] + square[k] for k in span]
            cube = [dot(square[k], rest[k]) for k in span]
            for k in span:
                c = lead[k]
                slope = 0.75 + 0.25 * c
                rest[k] = (0.25 * c * c) * rest[k] + slope * square[k] + 0.25 * cube[k]
                lead[k] = c * c * slope
            cross = [dot(part[k], rest[k]) for k in span]
            for k in span:
                grow = 1.0 + 0.5 * lead[k]
                part[k] = (0.5 * gain[k]) * rest[k] + grow * part[k] + 0.5 * cross[k]
                gain[k] = gain[k] * grow
        for k in span:
            over = lax.rsqrt(scale[k])
            push = proj[pl.ds(r0 + k, 1), :] + proj[pl.ds(regions + r0 + k, 1), :]
            push = jnp.broadcast_to(push, (8, ensemble))
            halfway = (gain[k] * push + dot(push, part[k])) * over
            mean = (gain[k] * halfway + dot(halfway, part[k])) * over
            root = (gain[k] * identity + part[k]) * over
            across = (ensemble - 1.0) ** 0.5 * root - identity + mean[0:1]
            at = pl.multiple_of((r0 + k) * ensemble, ensemble)
            mix[pl.ds(at, ensemble), :] = across.T.astype(jnp.bfloat16)

    def quad(i, carry):
        transform(4 * i, 4)
        return carry

    lax.fori_loop(0, regions // 4, quad, 0)

    def increments(direction, target):
        def one(i, carry):
            block = state_in[direction, i].astype(jnp.float32)
            at = pl.multiple_of(i * state_rows, state_rows)
            for r in range(regions):
                scaled[pl.ds(at, state_rows), r * ensemble : (r + 1) * ensemble] = (
                    block * taper_ref[r, direction * CAP + i]
                ).astype(jnp.bfloat16)
            return carry

        lax.fori_loop(0, CAP, one, 0)
        made = jnp.dot(scaled[...], mix[...], preferred_element_type=jnp.float32)
        target[direction] = made.astype(jnp.bfloat16).reshape(CAP, state_rows, ensemble)

    def send_share(direction, device):
        copy_from(direction, state_out, state_in, state_send, state_recv, device).wait()
        increments(direction, share_out)
        copy_to(direction, share_out, share_in, share_send, share_recv, device).start()

    each(corner, send_share)
    each(edge, send_share)
    increments(OWN, share_in)

    def take_share(direction, device):
        copy_from(direction, share_out, share_in, share_send, share_recv, device).wait()

    each(edge, take_share)
    each(corner, take_share)
    for direction in range(NEAR):
        if direction // 3 != 1:
            exists, _ = peer(direction)

            @pl.when(jnp.logical_not(exists))
            def _():
                share_in[direction] = jnp.zeros(share_in.shape[1:], share_in.dtype)

    def combine(b, carry):
        result = members_ref[b].astype(jnp.float32)
        for direction in range(NEAR):
            share = share_in[direction, back_ref[direction, b]].astype(jnp.float32)
            result = result + share * hit_ref[direction, b]
        out_ref[b] = result.astype(jnp.bfloat16)
        return carry

    lax.fori_loop(0, blocks, combine, 0)


def local(band_count, lon_count, members, obs_perts, innovations, lists, placement, obs_taper, state_taper):
    block_count, state_rows, ensemble = members.shape
    obs_rows = obs_perts.shape[1]
    regions, list_len = lists.shape
    entries = regions * list_len
    pool = NEAR * CAP
    band_here = lax.axis_index("band")
    lon_here = lax.axis_index("lon")
    row_ids = jnp.take(placement, lists.reshape(-1), axis=0)
    holder = row_ids // block_count
    band_step = holder // lon_count - band_here
    lon_step = (holder % lon_count - lon_here + 1) % lon_count - 1
    neighbour = (band_step + 1) * 3 + lon_step + 1
    place = neighbour * block_count + row_ids % block_count
    named = place[:, None] == jnp.arange(NEAR * block_count, dtype=jnp.int32)[None, :]
    used = jnp.any(named, axis=0).reshape(NEAR, block_count)
    used_float = used.astype(jnp.float32)
    before = jnp.triu(jnp.ones((block_count, block_count), jnp.float32), 1)
    order = jnp.dot(used_float, before).astype(jnp.int32)
    caps = jnp.arange(CAP, dtype=jnp.int32)
    chosen = ((order[:, None, :] == caps[None, :, None]) & used[:, None, :]).astype(jnp.float32)
    block_ids = jnp.arange(block_count, dtype=jnp.float32)
    request = jnp.sum(chosen * block_ids, axis=2)
    slot_id = (order + CAP * jnp.arange(NEAR, dtype=jnp.int32)[:, None]).reshape(-1)
    slot = jnp.max(jnp.where(named, slot_id[None, :], 0), axis=1)
    slot_hot = (slot[:, None] == jnp.arange(pool, dtype=jnp.int32)[None, :]).astype(jnp.float32)
    slot_hot = slot_hot.reshape(regions, list_len, pool)

    lanes = 128
    innov = jnp.pad(innovations.astype(jnp.float32), ((0, 0), (0, lanes - obs_rows)))
    asked = jnp.pad(request[:, None, :], ((0, 0), (0, 7), (0, lanes - CAP)))
    message = jnp.concatenate(
        [jnp.broadcast_to(innov[None], (NEAR, block_count, lanes)), asked], axis=1
    )
    vmem = pl.BlockSpec(memory_space=pltpu.VMEM)
    smem = pl.BlockSpec(memory_space=pltpu.SMEM)
    got = pl.pallas_call(
        functools.partial(ask_kernel, band_count, lon_count),
        out_shape=jax.ShapeDtypeStruct(message.shape, jnp.float32),
        in_specs=[vmem],
        out_specs=vmem,
        scratch_shapes=[pltpu.SemaphoreType.DMA((NEAR,)), pltpu.SemaphoreType.DMA((NEAR,))],
        compiler_params=pltpu.CompilerParams(
            collective_id=0, has_side_effects=True, vmem_limit_bytes=16 * 2**20
        ),
    )(message)
    given = got[:, block_count, :CAP].astype(jnp.int32)
    ids = jnp.clip(given, 0, block_count - 1)
    match = given[:, None, :] == jnp.arange(block_count, dtype=jnp.int32)[None, :, None]
    back = jnp.max(jnp.where(match, caps[None, None, :], 0), axis=2)
    hit = jnp.any(match, axis=2).astype(jnp.float32)

    high = lax.Precision.HIGHEST
    weights = jnp.einsum("rjq,rjp->rqp", slot_hot, obs_taper, precision=high)
    tapers = jnp.sum(slot_hot * state_taper[:, :, None], axis=1)
    innov_pool = jnp.einsum("nib,nbp->nip", chosen, got[:, :block_count, :obs_rows])
    push = weights.reshape(regions, NEAR, CAP, obs_rows) * innov_pool[None]

    def by_neighbour(a):
        return a.reshape(regions, NEAR, CAP * obs_rows).transpose(1, 0, 2)

    weights = by_neighbour(weights)
    push = by_neighbour(push)
    push_high = push.astype(jnp.bfloat16)
    push_low = (push - push_high.astype(jnp.float32)).astype(jnp.bfloat16)
    push = jnp.concatenate([push_high, push_low], axis=1)

    obs_pool = pltpu.VMEM((NEAR, CAP * obs_rows, ensemble), jnp.bfloat16)
    state_pool = pltpu.VMEM((NEAR, CAP, state_rows, ensemble), jnp.bfloat16)
    sems = pltpu.SemaphoreType.DMA((NEAR,))
    return pl.pallas_call(
        functools.partial(analysis_kernel, band_count, lon_count),
        out_shape=jax.ShapeDtypeStruct(members.shape, members.dtype),
        in_specs=[smem, smem, smem, smem, vmem, vmem, vmem, vmem],
        out_specs=vmem,
        scratch_shapes=[
            obs_pool,
            obs_pool,
            state_pool,
            state_pool,
            state_pool,
            state_pool,
            pltpu.VMEM((regions, ensemble, ensemble), jnp.float32),
            pltpu.VMEM((ensemble, CAP * obs_rows), jnp.float32),
            pltpu.VMEM((2 * regions, ensemble), jnp.float32),
            pltpu.VMEM((regions * ensemble, ensemble), jnp.bfloat16),
            pltpu.VMEM((CAP * state_rows, regions * ensemble), jnp.bfloat16),
            sems,
            sems,
            sems,
            sems,
            sems,
            sems,
        ],
        compiler_params=pltpu.CompilerParams(
            collective_id=1, has_side_effects=True, vmem_limit_bytes=56 * 2**20
        ),
    )(ids, back, hit, tapers, members, obs_perts, weights, push)


def solution(mesh):
    in_specs = (
        P(("band", "lon"), None, None),
        P(("band", "lon"), None, None),
        P(("band", "lon"), None),
        P(("band", "lon"), None),
        P(),
        P(("band", "lon"), None, None),
        P(("band", "lon"), None),
    )
    out_specs = P(("band", "lon"), None, None)
    body = functools.partial(local, mesh.shape["band"], mesh.shape["lon"])
    return jax.shard_map(body, mesh=mesh, in_specs=in_specs, out_specs=out_specs, check_vma=False)
```

time: 586 us -> 173 us (0.30)
  the two profiles are of different devices: /device:TPU:6 before, /device:TPU:0 now
where the time goes in v1:
time: 173 us
  Pallas kernels  160 us (92%)
  local copies, waits for them, and re-layouts  7.2 us (4%)
  other arithmetic  4.92 us (3%)
    pallas_call x1, Pallas kernels, local(): pl.pallas_call(functools.partial(analysis_kernel, band_count, lon_count),...  150 us
    pallas_call x1, Pallas kernels, local(): pl.pallas_call(functools.partial(ask_kernel, band_count, lon_count), out_...  9.28 us

profile of v1, /device:TPU:0, one launch (start us, length us, event | category | flops | bytes accessed | tf_op | source)
XLA Modules:
  0.0 172.8 jit_solution(139060031938378716)
XLA Ops:
  0.0 0.0 copy-start
  0.0 0.0 copy-start.3
  0.0 0.8 reshape.155
  0.9 0.0 copy-done.1
  0.9 3.1 %gather_fusion = s32[512]{0:T(512)S(1)} fusion(s32[1536]{0:T(1024)S(1)} %copy-done.1, s32[1024]{0:T(1024)S(1)} %pad_clamp_fusion), kind=kCustom, calls=%fused_computation | custom fusion | bytes 6144 | tf_op jit(solution)/shard_map/jit(_take)/gather | solution.py:319
  4.0 0.0 copy-done.2
  4.0 0.1 reshape.154
  4.2 0.2 fusion
  4.3 0.1 reshape.156
  4.4 0.0 copy-done.3
  4.4 0.1 copy.23
  4.5 0.1 broadcast_add_fusion
  4.6 0.1 broadcast_in_dim.68
  4.8 0.2 select_reduce_fusion
  5.0 0.1 eq.72
  5.1 0.0 copy-done.4
  5.1 0.8 select_reduce_fusion.1.taper_ref
  5.9 0.1 select_reduce_fusion.3
  6.0 9.3 %shard_map.73 = f32[9,56,128]{2,1,0:T(8,128)S(1)} custom-call(f32[9,56,128]{2,1,0:T(8,128)S(1)} %select_maximum_fusion.ask_ref), custom_call_target="tpu_custom_call" | custom-call | tf_op jit(solution)/shard_map/pallas_call | solution.py:347
  15.3 0.1 fusion.5
  15.5 0.1 mul.58
  15.6 0.1 fusion.8
  15.7 0.7 select_reduce_fusion.2.back_ref
  16.4 0.6 fusion.18.ids_ref
  17.0 0.6 convert_element_type.31.hit_ref
  17.6 0.7 fusion.2
  18.3 0.3 reshape.157
  18.5 0.1 fusion.7
  18.6 0.8 bitcast_convert_fusion
  19.4 0.7 pad_maximum_fusion.push_ref
  20.1 150.4 %shard_map.74 = bf16[48,48,256]{2,1,0:T(8,128)(2,1)} custom-call(s32[9,16]{1,0:T(8,128)} %fusion.18.ids_ref, s32[9,48]{1,0:T(8,128)} %select_reduce_fusion.2.back_ref, f32[9,48]{1,0:T(8,128)} %convert_element_type.31.hit_ref, f32[8,144]{1,0:T(8,128)} %select_reduce_fusion.1.taper_ref, bf16[48,48,256]{2,1,0:T(8,128)(2,1)} %members_ref.1, ...), custom_call_target="tpu_custom_call" | custom-call | tf_op jit(solution)/shard_map/pallas_call | solution.py:381
  170.5 2.4 %copy.43 = bf16[48,48,256]{2,1,0:T(8,128)(2,1)} copy(bf16[48,48,256]{2,1,0:T(8,128)(2,1)} %shard_map.74) | data formatting | bytes 2359296
  (14 shorter events, 0.1 us)
Async XLA Ops:
  0.0 17.6 %copy-start = (f32[8,64,32]{1,2,0:T(8,128)S(1)}, f32[8,64,32]{1,2,0:T(8,128)}, u32[]{:S(2)}) copy-start(f32[8,64,32]{1,2,0:T(8,128)} %param.12) | copy-start | bytes 196612
  0.0 4.0 %copy-start.2 = (s32[8,64]{1,0:T(8,128)S(1)}, s32[8,64]{1,0:T(8,128)}, u32[]{:S(2)}) copy-start(s32[8,64]{1,0:T(8,128)} %param.10) | copy-start | bytes 6148
  0.0 5.1 %copy-start.4 = (f32[8,64]{1,0:T(8,128)S(1)}, f32[8,64]{1,0:T(8,128)}, u32[]{:S(2)}) copy-start(f32[8,64]{1,0:T(8,128)} %param.13) | copy-start | bytes 6148
  0.0 0.9 copy-start.1
  0.0 4.4 %copy-start.3 = (bf16[48,32]{0,1:T(8,128)(2,1)S(1)}, bf16[48,32]{0,1:T(8,128)(2,1)}, u32[]{:S(2)}) copy-start(bf16[48,32]{0,1:T(8,128)(2,1)} %param.9) | copy-start | bytes 9220
